TPU v7x, 128 devices: a whole 4x4x4 slice. The times are simulated.
128 devices in a mesh: grp: 4 (over x), dev: 32 (over y, z, core).
Axes of the slice: x: 4, y: 4, z: 4, core: 2. Of those that a mesh axis runs over, the one named last changes fastest.
Arguments:
- pair_owner: int32 [8192, 2], P(('grp', 'dev')), may hold values from 0 to 127, all different within a row; in each aligned block of 64 rows (0 to 63, 64 to 127, ...) at most 2 rows name the same one
- pair_atom: int32 [8192, 2], P(('grp', 'dev')), may hold values from 0 to 95
- integrals: bfloat16 [8192, 128, 1024], P(('grp', 'dev')), may hold values from -1.5 to 1.5
- metric_inverse: bfloat16 [8192, 128, 128], P(('grp', 'dev')), may hold values from -0.3 to 3, as said below
- density: bfloat16 [12288, 1024], P(('grp', 'dev')), may hold values from -0.1796875 to 0.1796875
Outputs:
- exchange_diag: float32 [12288, 1024], P(('grp', 'dev'))
Inputs may be any that keep to these rules, and one draw needn't show every extreme that they name: `pair_owner`: the two entries of a row differ. Among the 128 entries of one device's rows, no device is named more than 2 times, and some device is named exactly 2 times in every draw. `metric_inverse`: each pair's matrix is symmetric.
All inputs are finite; a program needn't handle non-finite values.
Results may differ from a plain program's by a relative error of at most 0.0039.
Values may be sent and summed in bfloat16 or wider, within the bound.
A program may use at most 192 MiB of HBM per device.

v0:
```python
import itertools

import jax
import jax.numpy as jnp
from jax import lax
from jax.experimental import pallas as pl
from jax.experimental.pallas import tpu as pltpu
from jax.sharding import PartitionSpec as P

NB = 32
NFIT = 128
ATOMS = 96
PAIRS = 64
DEVS = 128
GROUP = 4
GROUPS = PAIRS // GROUP
BUFFERS = 4
EARLY = 9
EXPAND = 16
PITCH = 33
BF16 = jnp.bfloat16
F32 = jnp.float32
MESH = pl.DeviceIdType.MESH
NT = (((1,), (1,)), ((), ()))


OFFSETS = sorted(
    (o for o in itertools.product(range(4), range(4), range(4), range(2)) if any(o)),
    key=lambda o: (-sum(min(v, 4 - v) for v in o[:3]), -o[3]),
)


def place(t):
    return (t // 32, t % 32)


def my_index():
    return lax.axis_index("grp") * 32 + lax.axis_index("dev")


def farthest_first(me):
    x, y, z, core = me // 32, (me // 8) % 4, (me // 2) % 4, me % 2
    for dx, dy, dz, dc in OFFSETS:
        yield ((x + dx) % 4) * 32 + ((y + dy) % 4) * 8 + ((z + dz) % 4) * 2 + (core + dc) % 2


def start_swap(me, send, recv, send_sem, recv_sem):
    pltpu.make_async_copy(send.at[me], recv.at[me], recv_sem).start()
    for t in farthest_first(me):
        pltpu.make_async_remote_copy(
            src_ref=send.at[t], dst_ref=recv.at[me], send_sem=send_sem, recv_sem=recv_sem,
            device_id=place(t), device_id_type=MESH,
        ).start()


def wait_swap(send, recv, send_sem, recv_sem):
    pltpu.make_async_copy(recv, recv, recv_sem).wait()
    others = send.at[pl.ds(0, DEVS - 1)]
    pltpu.make_async_copy(others, others, send_sem).wait()


def spread(block, lane_group):
    return jnp.concatenate([jnp.where(lane_group == g, block, 0.0) for g in range(4)], axis=0).astype(BF16)


def eightfold(e_ref, keep):
    rows = [jnp.where(keep, jnp.broadcast_to(e_ref[c : c + 1, :], (8, 256)), 0.0) for c in range(NB)]
    return jnp.concatenate(rows, axis=0).astype(BF16)


def apply_block(k, w_ref, g, rows, y_ref, where_a, where_c):
    w = jnp.concatenate(
        [
            jnp.concatenate(
                [w_ref[g, rows, where_a(ac, a) * 128 : (where_a(ac, a) + 1) * 128] for a in range(8)], axis=0
            )
            for ac in range(4)
        ],
        axis=1,
    )
    y = jnp.dot(k, w, preferred_element_type=F32)
    for c in range(NB):
        at = where_c(c)
        y_ref[rows, at * 128 : (at + 1) * 128] = jnp.concatenate(
            [y[c * 8 : (c + 1) * 8, ac * 128 : (ac + 1) * 128] for ac in range(4)], axis=0
        ).astype(BF16)


def item_tables(owner_ref, atom_ref, tables):
    items = 2 * PAIRS
    lane = lax.broadcasted_iota(jnp.int32, (PAIRS, items), 1)
    here = lane % PAIRS == lax.broadcasted_iota(jnp.int32, (PAIRS, items), 0)

    def as_row(ref):
        both = jnp.where(lane < PAIRS, ref[:, 0:1], ref[:, 1:2])
        return jnp.sum(jnp.where(here, both, 0), axis=0, keepdims=True)

    owner = as_row(owner_ref)
    column = jnp.concatenate([owner_ref[:, 0:1], owner_ref[:, 1:2]], axis=0)
    item = lax.broadcasted_iota(jnp.int32, (items, items), 0)
    across = lax.broadcasted_iota(jnp.int32, (items, items), 1)
    slot = jnp.sum(jnp.where((column == owner) & (item < across), 1, 0), axis=0, keepdims=True)
    named = column == across
    first = jnp.min(jnp.where(named, item, items), axis=0, keepdims=True)
    last = jnp.max(jnp.where(named, item, -1), axis=0, keepdims=True)
    tables[0:1, :] = owner * ATOMS + as_row(atom_ref)
    tables[1:2, :] = owner
    tables[2:3, :] = slot
    tables[3:4, :] = first
    tables[4:5, :] = jnp.where(last > first, last, items)
    tables[5:8, :] = jnp.zeros((3, items), jnp.int32)


def exchange_kernel(
    owner_ref, atom_ref, integrals, metric, density, total,
    tables, scalars, req, dens, outgoing, landed, outbox, returned, rows32, chosen,
    q_buf, m_buf, z_ref, fw, qw, x_ref, r_ref, e1_ref, e2_ref, terms,
    sems, q_sems, m_sems,
):
    me = my_index()

    def load(g, buffer):
        return (
            pltpu.make_async_copy(integrals.at[pl.ds(g * GROUP, GROUP)], q_buf.at[buffer], q_sems.at[buffer]),
            pltpu.make_async_copy(metric.at[pl.ds(g * GROUP, GROUP)], m_buf.at[buffer], m_sems.at[buffer]),
        )

    barrier = pltpu.get_barrier_semaphore()

    def signal(i, carry):
        pl.semaphore_signal(barrier, inc=1, device_id=place((me + i) % DEVS), device_id_type=MESH)
        return carry

    lax.fori_loop(1, DEVS, signal, 0)
    for g in range(BUFFERS):
        for copy in load(g, g):
            copy.start()
    density_copy = pltpu.make_async_copy(density, dens, sems.at[4])
    density_copy.start()
    item_tables(owner_ref, atom_ref, tables)
    table_copy = pltpu.make_async_copy(tables, scalars, sems.at[5])
    table_copy.start()
    pl.semaphore_wait(barrier, DEVS - 1)

    codes = tables.at[pl.ds(0, 1)]
    pltpu.make_async_copy(codes, req.at[pl.ds(me, 1)], sems.at[0]).start()
    for t in farthest_first(me):
        pltpu.make_async_remote_copy(
            src_ref=codes, dst_ref=req.at[pl.ds(me, 1)], send_sem=sems.at[1], recv_sem=sems.at[0],
            device_id=place(t), device_id_type=MESH,
        ).start()
    terms[2 * PAIRS] = jnp.zeros((8, 128), F32)

    def fit(g, carry):
        buffer = g % BUFFERS
        for copy in load(g, buffer):
            copy.wait()
        for p in range(GROUP):
            rows = slice(p * NB, (p + 1) * NB)
            for c in range(8):
                t = q_buf[buffer, p, :, c * 128 : (c + 1) * 128].T
                y = jnp.dot(t, m_buf[buffer, p], preferred_element_type=F32)
                for j in range(4):
                    m = 4 * c + j
                    at = (j * 8 + c) * PITCH
                    qw[g, rows, m * 128 : (m + 1) * 128] = t[j * NB : (j + 1) * NB]
                    z_ref[p, at : at + NB, :] = y[j * NB : (j + 1) * NB]
            for n in range(NB):
                fw[g, rows, n * 128 : (n + 1) * 128] = z_ref[p, pl.ds(n, NB, stride=PITCH), :].astype(BF16)

        @pl.when(g + BUFFERS < GROUPS)
        def _():
            for copy in load(g + BUFFERS, buffer):
                copy.start()

        return carry

    lax.fori_loop(0, EARLY, fit, 0)

    pltpu.make_async_copy(req, req, sems.at[0]).wait()
    density_copy.wait()
    local = req[...] - ATOMS * me
    mine = (local >= 0) & (local < ATOMS)
    coded = lax.broadcasted_iota(jnp.int32, (DEVS, 128), 1) * 128 + local
    first = jnp.min(jnp.where(mine, coded, 128 * 128 - 1), axis=1, keepdims=True) % 128
    last = jnp.max(jnp.where(mine, coded, 127), axis=1, keepdims=True) % 128
    atoms = lax.broadcasted_iota(jnp.int32, (DEVS, 128), 1)
    onehots = [jnp.where(atoms == atom, 1.0, 0.0) for atom in (first, last)]
    for c in range(2):
        picks = onehots[c][:, :ATOMS].astype(BF16)
        for part in range(8):
            rows32[pl.ds(8 * c + part, DEVS, stride=16), :] = jnp.dot(
                picks, dens[:, part * 128 : (part + 1) * 128], preferred_element_type=F32
            )
    outgoing[...] = rows32[...].reshape(DEVS, 16, 128).astype(BF16)
    start_swap(me, outgoing, landed, sems.at[2], sems.at[3])
    for c in range(2):
        chosen[c] = onehots[c].T.astype(BF16)
    others = req.at[pl.ds(0, DEVS - 1)]
    pltpu.make_async_copy(others, others, sems.at[1]).wait()
    table_copy.wait()
    lax.fori_loop(EARLY, GROUPS, fit, 0)
    wait_swap(outgoing, landed, sems.at[2], sems.at[3])

    lane256 = lax.broadcasted_iota(jnp.int32, (8, 256), 1)
    keep = lax.broadcasted_iota(jnp.int32, (8, 256), 0) == lane256 // NB
    lane_group = lax.broadcasted_iota(jnp.int32, (8, 128), 1) // NB
    tile8 = jnp.where(
        lax.broadcasted_iota(jnp.int32, (128, 256), 0) % NB == lax.broadcasted_iota(jnp.int32, (128, 256), 1) % NB,
        1.0, 0.0,
    ).astype(BF16)
    pick = jnp.where(
        lax.broadcasted_iota(jnp.int32, (NB, 128), 0) == lax.broadcasted_iota(jnp.int32, (NB, 128), 1) % NB, 1.0, 0.0
    ).astype(BF16)

    def fetched(item):
        both = landed[scalars[1, item]].astype(F32)
        return jnp.where(scalars[2, item] == 0, both[:8], both[8:])

    def expand(h, carry):
        firsts = [spread(fetched(h * EXPAND + p), lane_group) for p in range(EXPAND)]
        seconds = [spread(fetched(PAIRS + h * EXPAND + p), lane_group) for p in range(EXPAND)]
        e2 = jnp.dot(jnp.concatenate(seconds, axis=0), tile8, preferred_element_type=F32)
        e2_ref[pl.ds(h * EXPAND, EXPAND)] = e2.reshape(EXPAND, NB, 256)
        e1 = lax.dot_general(
            pick, jnp.concatenate([f for f in firsts for _ in range(8)], axis=0), NT, preferred_element_type=F32
        )
        for p in range(EXPAND):
            e1_ref[h * EXPAND + p] = e1[:, p * 256 : (p + 1) * 256]
        return carry

    lax.fori_loop(0, PAIRS // EXPAND, expand, 0)

    def contract(g, carry):
        for p in range(GROUP):
            rows = slice(p * NB, (p + 1) * NB)
            pair = g * GROUP + p
            apply_block(
                eightfold(e2_ref.at[pair], keep), qw, g, rows, x_ref,
                lambda ac, a: ac * 8 + a, lambda c: (c % 8) * 4 + c // 8,
            )
            apply_block(
                eightfold(e1_ref.at[pair], keep), fw, g, rows, r_ref, lambda ac, a: a * 4 + ac, lambda c: c
            )
        first_gram = lax.dot_general(fw[g], x_ref[...], NT, preferred_element_type=F32)
        second_gram = lax.dot_general(r_ref[...], qw[g], NT, preferred_element_type=F32)
        for side, gram in ((0, first_gram), (1, second_gram)):
            for p in range(GROUP):
                block = jnp.zeros((8, 128), F32)
                for k in range(4):
                    part = gram[p * NB + k * 8 : p * NB + (k + 1) * 8, :]
                    turn = ((k - p) % 4) * NB
                    block = jnp.where(lane_group == k, part if turn == 0 else pltpu.roll(part, turn, 1), block)
                terms[side * PAIRS + g * GROUP + p] = block
        return carry

    lax.fori_loop(0, GROUPS, contract, 0)

    def box(t, carry):
        both = jnp.concatenate([terms[scalars[3, t]], terms[scalars[4, t]]], axis=0)
        outbox[t] = both.astype(BF16)
        return carry

    lax.fori_loop(0, DEVS, box, 0, unroll=8)
    start_swap(me, outbox, returned, sems.at[6], sems.at[7])
    wait_swap(outbox, returned, sems.at[6], sems.at[7])
    rows32[...] = returned[...].astype(F32).reshape(DEVS * 16, 128)
    for part in range(8):
        acc = None
        for c in range(2):
            tile = rows32[pl.ds(8 * c + part, DEVS, stride=16), :].astype(BF16)
            term = jnp.dot(chosen[c, :ATOMS, :], tile, preferred_element_type=F32)
            acc = term if acc is None else acc + term
        total[:, part * 128 : (part + 1) * 128] = acc


def local(pair_owner, pair_atom, integrals, metric_inverse, density):
    vmem = pl.BlockSpec(memory_space=pltpu.VMEM)
    hbm = pl.BlockSpec(memory_space=pl.ANY)
    boxes = pltpu.VMEM((DEVS, 16, 128), BF16)
    wide = (GROUP * NB, NB * NFIT)
    return pl.pallas_call(
        exchange_kernel,
        out_shape=jax.ShapeDtypeStruct((ATOMS, NB * NB), F32),
        in_specs=[vmem, vmem, hbm, hbm, hbm],
        out_specs=vmem,
        scratch_shapes=[
            pltpu.VMEM((8, 2 * PAIRS), jnp.int32),
            pltpu.SMEM((8, 2 * PAIRS), jnp.int32),
            pltpu.VMEM((DEVS, 2 * PAIRS), jnp.int32),
            pltpu.VMEM((ATOMS, NB * NB), BF16),
            boxes, boxes, boxes, boxes,
            pltpu.VMEM((DEVS * 16, 128), F32),
            pltpu.VMEM((2, 128, DEVS), BF16),
            pltpu.VMEM((BUFFERS, GROUP, NFIT, NB * NB), BF16),
            pltpu.VMEM((BUFFERS, GROUP, NFIT, NFIT), BF16),
            pltpu.VMEM((GROUP, NB * PITCH, 128), F32),
            pltpu.VMEM((GROUPS, *wide), BF16),
            pltpu.VMEM((GROUPS, *wide), BF16),
            pltpu.VMEM(wide, BF16),
            pltpu.VMEM(wide, BF16),
            pltpu.VMEM((PAIRS, NB, 256), F32),
            pltpu.VMEM((PAIRS, NB, 256), F32),
            pltpu.VMEM((2 * PAIRS + 1, 8, 128), F32),
            pltpu.SemaphoreType.DMA((8,)),
            pltpu.SemaphoreType.DMA((BUFFERS,)),
            pltpu.SemaphoreType.DMA((BUFFERS,)),
        ],
        compiler_params=pltpu.CompilerParams(
            collective_id=0, has_side_effects=True, vmem_limit_bytes=58 * 2**20
        ),
        name="exchange",
    )(pair_owner, pair_atom, integrals, metric_inverse, density)


def solution(mesh):
    placed = (
        P(("grp", "dev"), None),
        P(("grp", "dev"), None),
        P(("grp", "dev"), None, None),
        P(("grp", "dev"), None, None),
        P(("grp", "dev"), None),
    )
    return jax.shard_map(
        local, mesh=mesh, in_specs=placed, out_specs=P(("grp", "dev"), None), check_vma=False
    )
```

profile of v0, /device:TPU:1, one launch (start us, length us, event | category | flops | bytes accessed | tf_op | source)
XLA Modules:
  0.0 68.1 jit_solution(810573985548564190)
XLA Ops:
  0.0 1.4 %copy.6.owner_ref = s32[64,2]{1,0:T(8,128)} copy(s32[64,2]{0,1:T(2,128)} %param.5) | data formatting | bytes 1024 | tf_op args[0]
  1.4 1.4 %copy.7.atom_ref = s32[64,2]{1,0:T(8,128)} copy(s32[64,2]{0,1:T(2,128)} %param.6) | data formatting | bytes 1024 | tf_op args[1]
  2.7 63.6 %exchange.1 = f32[96,1024]{1,0:T(8,128)} custom-call(s32[64,2]{1,0:T(8,128)} %copy.6.owner_ref, s32[64,2]{1,0:T(8,128)} %copy.7.atom_ref, bf16[64,128,1024]{2,1,0:T(8,128)(2,1)} %integrals.1, bf16[64,128,128]{2,1,0:T(8,128)(2,1)} %metric.1, bf16[96,1024]{1,0:T(8,128)(2,1)} %density.1), custom_call_target="tpu_custom_call" | custom-call | tf_op jit(solution)/shard_map/exchange/pallas_call | solution.py:282
  66.3 1.8 %copy.9 = f32[96,1024]{1,0:T(8,128)} copy(f32[96,1024]{1,0:T(8,128)} %exchange.1) | data formatting | bytes 786432
where the time goes:
time: 68.3 us; the launch traced here: 68.1 us
  Pallas kernels  63.6 us (93%)
  local copies, waits for them, and re-layouts  4.52 us (7%)
    pallas_call x1, Pallas kernels, local(): pl.pallas_call(exchange_kernel, out_shape=jax.ShapeDtypeStruct((ATOMS, NB...  63.6 us
    unnamed x3, local copies, waits for them, and re-layouts  4.52 us

commit v1 on v0

--- a/solution.py
+++ b/solution.py
@@ -16,7 +16,6 @@
 GROUPS = PAIRS // GROUP
 BUFFERS = 4
 EARLY = 9
-EXPAND = 16
 PITCH = 33
 BF16 = jnp.bfloat16
 F32 = jnp.float32
@@ -44,13 +43,15 @@
         yield ((x + dx) % 4) * 32 + ((y + dy) % 4) * 8 + ((z + dz) % 4) * 2 + (core + dc) % 2
 
 
-def start_swap(me, send, recv, send_sem, recv_sem):
-    pltpu.make_async_copy(send.at[me], recv.at[me], recv_sem).start()
+def start_swap(me, send, recv, send_sem, recv_sem, fill):
     for t in farthest_first(me):
+        fill(t)
         pltpu.make_async_remote_copy(
             src_ref=send.at[t], dst_ref=recv.at[me], send_sem=send_sem, recv_sem=recv_sem,
             device_id=place(t), device_id_type=MESH,
         ).start()
+    fill(me)
+    pltpu.make_async_copy(send.at[me], recv.at[me], recv_sem).start()
 
 
 def wait_swap(send, recv, send_sem, recv_sem):
@@ -88,17 +89,14 @@
 
 def item_tables(owner_ref, atom_ref, tables):
     items = 2 * PAIRS
-    lane = lax.broadcasted_iota(jnp.int32, (PAIRS, items), 1)
-    here = lane % PAIRS == lax.broadcasted_iota(jnp.int32, (PAIRS, items), 0)
 
     def as_row(ref):
-        both = jnp.where(lane < PAIRS, ref[:, 0:1], ref[:, 1:2])
-        return jnp.sum(jnp.where(here, both, 0), axis=0, keepdims=True)
+        return jnp.concatenate([ref[0:1, :], ref[1:2, :]], axis=1)
 
     owner = as_row(owner_ref)
-    column = jnp.concatenate([owner_ref[:, 0:1], owner_ref[:, 1:2]], axis=0)
     item = lax.broadcasted_iota(jnp.int32, (items, items), 0)
     across = lax.broadcasted_iota(jnp.int32, (items, items), 1)
+    column = jnp.sum(jnp.where(item == across, owner, 0), axis=1, keepdims=True)
     slot = jnp.sum(jnp.where((column == owner) & (item < across), 1, 0), axis=0, keepdims=True)
     named = column == across
     first = jnp.min(jnp.where(named, item, items), axis=0, keepdims=True)
@@ -114,7 +112,7 @@
 def exchange_kernel(
     owner_ref, atom_ref, integrals, metric, density, total,
     tables, scalars, req, dens, outgoing, landed, outbox, returned, rows32, chosen,
-    q_buf, m_buf, z_ref, fw, qw, x_ref, r_ref, e1_ref, e2_ref, terms,
+    q_buf, m_buf, z_ref, fw, qw, x_even, r_even, x_odd, r_odd, e1_even, e2_even, e1_odd, e2_odd, terms,
     sems, q_sems, m_sems,
 ):
     me = my_index()
@@ -127,11 +125,8 @@
 
     barrier = pltpu.get_barrier_semaphore()
 
-    def signal(i, carry):
-        pl.semaphore_signal(barrier, inc=1, device_id=place((me + i) % DEVS), device_id_type=MESH)
-        return carry
-
-    lax.fori_loop(1, DEVS, signal, 0)
+    for t in farthest_first(me):
+        pl.semaphore_signal(barrier, inc=1, device_id=place(t), device_id_type=MESH)
     for g in range(BUFFERS):
         for copy in load(g, g):
             copy.start()
@@ -192,8 +187,11 @@
             rows32[pl.ds(8 * c + part, DEVS, stride=16), :] = jnp.dot(
                 picks, dens[:, part * 128 : (part + 1) * 128], preferred_element_type=F32
             )
-    outgoing[...] = rows32[...].reshape(DEVS, 16, 128).astype(BF16)
-    start_swap(me, outgoing, landed, sems.at[2], sems.at[3])
+
+    def answer(t):
+        outgoing[t] = rows32[pl.ds(pl.multiple_of(t * 16, 16), 16), :].astype(BF16)
+
+    start_swap(me, outgoing, landed, sems.at[2], sems.at[3], answer)
     for c in range(2):
         chosen[c] = onehots[c].T.astype(BF16)
     others = req.at[pl.ds(0, DEVS - 1)]
@@ -217,33 +215,29 @@
         both = landed[scalars[1, item]].astype(F32)
         return jnp.where(scalars[2, item] == 0, both[:8], both[8:])
 
-    def expand(h, carry):
-        firsts = [spread(fetched(h * EXPAND + p), lane_group) for p in range(EXPAND)]
-        seconds = [spread(fetched(PAIRS + h * EXPAND + p), lane_group) for p in range(EXPAND)]
-        e2 = jnp.dot(jnp.concatenate(seconds, axis=0), tile8, preferred_element_type=F32)
-        e2_ref[pl.ds(h * EXPAND, EXPAND)] = e2.reshape(EXPAND, NB, 256)
-        e1 = lax.dot_general(
+    def expand(g, e1, e2):
+        firsts = [spread(fetched(g * GROUP + p), lane_group) for p in range(GROUP)]
+        seconds = [spread(fetched(PAIRS + g * GROUP + p), lane_group) for p in range(GROUP)]
+        e2[...] = jnp.dot(
+            jnp.concatenate(seconds, axis=0), tile8, preferred_element_type=F32
+        ).reshape(GROUP, NB, 256)
+        wide = lax.dot_general(
             pick, jnp.concatenate([f for f in firsts for _ in range(8)], axis=0), NT, preferred_element_type=F32
         )
-        for p in range(EXPAND):
-            e1_ref[h * EXPAND + p] = e1[:, p * 256 : (p + 1) * 256]
-        return carry
-
-    lax.fori_loop(0, PAIRS // EXPAND, expand, 0)
-
-    def contract(g, carry):
+        for p in range(GROUP):
+            e1[p] = wide[:, p * 256 : (p + 1) * 256]
+
+    def apply(g, e1, e2, x, r):
         for p in range(GROUP):
             rows = slice(p * NB, (p + 1) * NB)
-            pair = g * GROUP + p
             apply_block(
-                eightfold(e2_ref.at[pair], keep), qw, g, rows, x_ref,
-                lambda ac, a: ac * 8 + a, lambda c: (c % 8) * 4 + c // 8,
+                eightfold(e2.at[p], keep), qw, g, rows, x, lambda ac, a: ac * 8 + a, lambda c: (c % 8) * 4 + c // 8
             )
-            apply_block(
-                eightfold(e1_ref.at[pair], keep), fw, g, rows, r_ref, lambda ac, a: a * 4 + ac, lambda c: c
-            )
-        first_gram = lax.dot_general(fw[g], x_ref[...], NT, preferred_element_type=F32)
-        second_gram = lax.dot_general(r_ref[...], qw[g], NT, preferred_element_type=F32)
+            apply_block(eightfold(e1.at[p], keep), fw, g, rows, r, lambda ac, a: a * 4 + ac, lambda c: c)
+
+    def contract(g, x, r):
+        first_gram = lax.dot_general(fw[g], x[...], NT, preferred_element_type=F32)
+        second_gram = lax.dot_general(r[...], qw[g], NT, preferred_element_type=F32)
         for side, gram in ((0, first_gram), (1, second_gram)):
             for p in range(GROUP):
                 block = jnp.zeros((8, 128), F32)
@@ -252,17 +246,30 @@
                     turn = ((k - p) % 4) * NB
                     block = jnp.where(lane_group == k, part if turn == 0 else pltpu.roll(part, turn, 1), block)
                 terms[side * PAIRS + g * GROUP + p] = block
+
+    expand(0, e1_even, e2_even)
+    apply(0, e1_even, e2_even, x_even, r_even)
+
+    def two_groups(h, carry):
+        g = 2 * h
+        expand(g + 1, e1_odd, e2_odd)
+        contract(g, x_even, r_even)
+        apply(g + 1, e1_odd, e2_odd, x_odd, r_odd)
+        expand(g + 2, e1_even, e2_even)
+        contract(g + 1, x_odd, r_odd)
+        apply(g + 2, e1_even, e2_even, x_even, r_even)
         return carry
 
-    lax.fori_loop(0, GROUPS, contract, 0)
-
-    def box(t, carry):
-        both = jnp.concatenate([terms[scalars[3, t]], terms[scalars[4, t]]], axis=0)
-        outbox[t] = both.astype(BF16)
-        return carry
-
-    lax.fori_loop(0, DEVS, box, 0, unroll=8)
-    start_swap(me, outbox, returned, sems.at[6], sems.at[7])
+    lax.fori_loop(0, GROUPS // 2 - 1, two_groups, 0)
+    expand(GROUPS - 1, e1_odd, e2_odd)
+    contract(GROUPS - 2, x_even, r_even)
+    apply(GROUPS - 1, e1_odd, e2_odd, x_odd, r_odd)
+    contract(GROUPS - 1, x_odd, r_odd)
+
+    def box(t):
+        outbox[t] = jnp.concatenate([terms[scalars[3, t]], terms[scalars[4, t]]], axis=0).astype(BF16)
+
+    start_swap(me, outbox, returned, sems.at[6], sems.at[7], box)
     wait_swap(outbox, returned, sems.at[6], sems.at[7])
     rows32[...] = returned[...].astype(F32).reshape(DEVS * 16, 128)
     for part in range(8):
@@ -297,10 +304,8 @@
             pltpu.VMEM((GROUP, NB * PITCH, 128), F32),
             pltpu.VMEM((GROUPS, *wide), BF16),
             pltpu.VMEM((GROUPS, *wide), BF16),
-            pltpu.VMEM(wide, BF16),
-            pltpu.VMEM(wide, BF16),
-            pltpu.VMEM((PAIRS, NB, 256), F32),
-            pltpu.VMEM((PAIRS, NB, 256), F32),
+            *[pltpu.VMEM(wide, BF16)] * 4,
+            *[pltpu.VMEM((GROUP, NB, 256), F32)] * 4,
             pltpu.VMEM((2 * PAIRS + 1, 8, 128), F32),
             pltpu.SemaphoreType.DMA((8,)),
             pltpu.SemaphoreType.DMA((BUFFERS,)),
@@ -310,7 +315,7 @@
             collective_id=0, has_side_effects=True, vmem_limit_bytes=58 * 2**20
         ),
         name="exchange",
-    )(pair_owner, pair_atom, integrals, metric_inverse, density)
+    )(pair_owner.T, pair_atom.T, integrals, metric_inverse, density)
 
 
 def solution(mesh):

time: 68.3 us -> 60.2 us (0.88)
  Pallas kernels: 63.6 us -> 58.3 us
  local copies, waits for them, and re-layouts: 4.52 us -> 1.77 us
    pallas_call x1, Pallas kernels: 63.6 us -> 58.3 us  [local(): pl.pallas_call(exchange_kernel, out_shape=jax.ShapeDtypeStruct((ATOMS, NB...]
    unnamed x3 -> x1, local copies, waits for them, and re-layouts: 4.52 us -> 1.77 us
where the time goes in v1:
time: 60.2 us; the launch traced here: 60.1 us
  Pallas kernels  58.3 us (97%)
  local copies, waits for them, and re-layouts  1.77 us (3%)
    pallas_call x1, Pallas kernels, local(): pl.pallas_call(exchange_kernel, out_shape=jax.ShapeDtypeStruct((ATOMS, NB...  58.3 us
    unnamed x1, local copies, waits for them, and re-layouts  1.77 us

profile of v1, /device:TPU:1, one launch (start us, length us, event | category | flops | bytes accessed | tf_op | source)
XLA Modules:
  0.0 60.1 jit_solution(9485958401108434956)
XLA Ops:
  0.0 58.3 %exchange.1 = f32[96,1024]{1,0:T(8,128)} custom-call(s32[2,64]{1,0:T(2,128)} %bitcast.2, s32[2,64]{1,0:T(2,128)} %bitcast.3, bf16[64,128,1024]{2,1,0:T(8,128)(2,1)} %integrals.1, bf16[64,128,128]{2,1,0:T(8,128)(2,1)} %metric.1, bf16[96,1024]{1,0:T(8,128)(2,1)} %density.1), custom_call_target="tpu_custom_call" | custom-call | tf_op jit(solution)/shard_map/exchange/pallas_call | solution.py:289
  58.3 1.8 %copy.7 = f32[96,1024]{1,0:T(8,128)} copy(f32[96,1024]{1,0:T(8,128)} %exchange.1) | data formatting | bytes 786432

commit v2 on v1

--- a/solution.py
+++ b/solution.py
@@ -15,7 +15,8 @@
 GROUP = 4
 GROUPS = PAIRS // GROUP
 BUFFERS = 4
-EARLY = 9
+EARLY = 6
+BOX = 24
 PITCH = 33
 BF16 = jnp.bfloat16
 F32 = jnp.float32
@@ -54,8 +55,11 @@
     pltpu.make_async_copy(send.at[me], recv.at[me], recv_sem).start()
 
 
-def wait_swap(send, recv, send_sem, recv_sem):
+def wait_received(recv, recv_sem):
     pltpu.make_async_copy(recv, recv, recv_sem).wait()
+
+
+def wait_sent(send, send_sem):
     others = send.at[pl.ds(0, DEVS - 1)]
     pltpu.make_async_copy(others, others, send_sem).wait()
 
@@ -110,10 +114,10 @@
 
 
 def exchange_kernel(
-    owner_ref, atom_ref, integrals, metric, density, total,
-    tables, scalars, req, dens, outgoing, landed, outbox, returned, rows32, chosen,
+    owners, atoms, integrals, metric, density, total,
+    owner_ref, atom_ref, tables, scalars, req, dens, outgoing, landed, outbox, returned, rows32, chosen,
     q_buf, m_buf, z_ref, fw, qw, x_even, r_even, x_odd, r_odd, e1_even, e2_even, e1_odd, e2_odd, terms,
-    sems, q_sems, m_sems,
+    sems, index_sems, q_sems, m_sems,
 ):
     me = my_index()
 
@@ -123,6 +127,12 @@
             pltpu.make_async_copy(metric.at[pl.ds(g * GROUP, GROUP)], m_buf.at[buffer], m_sems.at[buffer]),
         )
 
+    index_copies = [
+        pltpu.make_async_copy(owners, owner_ref, index_sems.at[0]),
+        pltpu.make_async_copy(atoms, atom_ref, index_sems.at[1]),
+    ]
+    for copy in index_copies:
+        copy.start()
     barrier = pltpu.get_barrier_semaphore()
 
     for t in farthest_first(me):
@@ -132,6 +142,8 @@
             copy.start()
     density_copy = pltpu.make_async_copy(density, dens, sems.at[4])
     density_copy.start()
+    for copy in index_copies:
+        copy.wait()
     item_tables(owner_ref, atom_ref, tables)
     table_copy = pltpu.make_async_copy(tables, scalars, sems.at[5])
     table_copy.start()
@@ -172,33 +184,31 @@
 
     lax.fori_loop(0, EARLY, fit, 0)
 
-    pltpu.make_async_copy(req, req, sems.at[0]).wait()
+    wait_received(req, sems.at[0])
     density_copy.wait()
     local = req[...] - ATOMS * me
     mine = (local >= 0) & (local < ATOMS)
     coded = lax.broadcasted_iota(jnp.int32, (DEVS, 128), 1) * 128 + local
     first = jnp.min(jnp.where(mine, coded, 128 * 128 - 1), axis=1, keepdims=True) % 128
     last = jnp.max(jnp.where(mine, coded, 127), axis=1, keepdims=True) % 128
-    atoms = lax.broadcasted_iota(jnp.int32, (DEVS, 128), 1)
-    onehots = [jnp.where(atoms == atom, 1.0, 0.0) for atom in (first, last)]
+    local_atom = lax.broadcasted_iota(jnp.int32, (DEVS, 128), 1)
+    onehots = [jnp.where(local_atom == atom, 1.0, 0.0) for atom in (first, last)]
     for c in range(2):
         picks = onehots[c][:, :ATOMS].astype(BF16)
         for part in range(8):
-            rows32[pl.ds(8 * c + part, DEVS, stride=16), :] = jnp.dot(
+            rows32[pl.ds(8 * c + part, DEVS, stride=BOX), :] = jnp.dot(
                 picks, dens[:, part * 128 : (part + 1) * 128], preferred_element_type=F32
             )
 
     def answer(t):
-        outgoing[t] = rows32[pl.ds(pl.multiple_of(t * 16, 16), 16), :].astype(BF16)
+        outgoing[t] = rows32[pl.ds(pl.multiple_of(t * BOX, 8), 16), :].astype(BF16)
 
     start_swap(me, outgoing, landed, sems.at[2], sems.at[3], answer)
     for c in range(2):
         chosen[c] = onehots[c].T.astype(BF16)
-    others = req.at[pl.ds(0, DEVS - 1)]
-    pltpu.make_async_copy(others, others, sems.at[1]).wait()
     table_copy.wait()
     lax.fori_loop(EARLY, GROUPS, fit, 0)
-    wait_swap(outgoing, landed, sems.at[2], sems.at[3])
+    wait_received(landed, sems.at[3])
 
     lane256 = lax.broadcasted_iota(jnp.int32, (8, 256), 1)
     keep = lax.broadcasted_iota(jnp.int32, (8, 256), 0) == lane256 // NB
@@ -270,34 +280,40 @@
         outbox[t] = jnp.concatenate([terms[scalars[3, t]], terms[scalars[4, t]]], axis=0).astype(BF16)
 
     start_swap(me, outbox, returned, sems.at[6], sems.at[7], box)
-    wait_swap(outbox, returned, sems.at[6], sems.at[7])
-    rows32[...] = returned[...].astype(F32).reshape(DEVS * 16, 128)
+    wait_received(returned, sems.at[7])
+    for t in range(DEVS):
+        rows32[t * BOX : t * BOX + 16, :] = returned[t].astype(F32)
     for part in range(8):
         acc = None
         for c in range(2):
-            tile = rows32[pl.ds(8 * c + part, DEVS, stride=16), :].astype(BF16)
+            tile = rows32[pl.ds(8 * c + part, DEVS, stride=BOX), :].astype(BF16)
             term = jnp.dot(chosen[c, :ATOMS, :], tile, preferred_element_type=F32)
             acc = term if acc is None else acc + term
         total[:, part * 128 : (part + 1) * 128] = acc
+    wait_sent(req, sems.at[1])
+    wait_sent(outgoing, sems.at[2])
+    wait_sent(outbox, sems.at[6])
 
 
 def local(pair_owner, pair_atom, integrals, metric_inverse, density):
     vmem = pl.BlockSpec(memory_space=pltpu.VMEM)
-    hbm = pl.BlockSpec(memory_space=pl.ANY)
+    hbm = pl.BlockSpec(memory_space=pltpu.HBM)
     boxes = pltpu.VMEM((DEVS, 16, 128), BF16)
     wide = (GROUP * NB, NB * NFIT)
     return pl.pallas_call(
         exchange_kernel,
         out_shape=jax.ShapeDtypeStruct((ATOMS, NB * NB), F32),
-        in_specs=[vmem, vmem, hbm, hbm, hbm],
+        in_specs=[hbm] * 5,
         out_specs=vmem,
         scratch_shapes=[
+            pltpu.VMEM((2, PAIRS), jnp.int32),
+            pltpu.VMEM((2, PAIRS), jnp.int32),
             pltpu.VMEM((8, 2 * PAIRS), jnp.int32),
             pltpu.SMEM((8, 2 * PAIRS), jnp.int32),
             pltpu.VMEM((DEVS, 2 * PAIRS), jnp.int32),
             pltpu.VMEM((ATOMS, NB * NB), BF16),
             boxes, boxes, boxes, boxes,
-            pltpu.VMEM((DEVS * 16, 128), F32),
+            pltpu.VMEM((DEVS * BOX, 128), F32),
             pltpu.VMEM((2, 128, DEVS), BF16),
             pltpu.VMEM((BUFFERS, GROUP, NFIT, NB * NB), BF16),
             pltpu.VMEM((BUFFERS, GROUP, NFIT, NFIT), BF16),
@@ -308,6 +324,7 @@
             *[pltpu.VMEM((GROUP, NB, 256), F32)] * 4,
             pltpu.VMEM((2 * PAIRS + 1, 8, 128), F32),
             pltpu.SemaphoreType.DMA((8,)),
+            pltpu.SemaphoreType.DMA((2,)),
             pltpu.SemaphoreType.DMA((BUFFERS,)),
             pltpu.SemaphoreType.DMA((BUFFERS,)),
         ],

time: 60.2 us -> 58.5 us (0.972)
  Pallas kernels: 58.3 us -> 56.6 us
    pallas_call x1, Pallas kernels: 58.3 us -> 56.6 us  [local(): pl.pallas_call(exchange_kernel, out_shape=jax.ShapeDtypeStruct((ATOMS, NB...]
where the time goes in v2:
time: 58.5 us; the launch traced here: 58.4 us
  Pallas kernels  56.6 us (97%)
  local copies, waits for them, and re-layouts  1.77 us (3%)
    pallas_call x1, Pallas kernels, local(): pl.pallas_call(exchange_kernel, out_shape=jax.ShapeDtypeStruct((ATOMS, NB...  56.6 us
    unnamed x1, local copies, waits for them, and re-layouts  1.77 us

profile of v2, /device:TPU:1, one launch (start us, length us, event | category | flops | bytes accessed | tf_op | source)
XLA Modules:
  0.0 58.4 jit_solution(68876255122235746)
XLA Ops:
  0.0 56.6 %exchange.1 = f32[96,1024]{1,0:T(8,128)} custom-call(s32[2,64]{1,0:T(2,128)} %bitcast.2, s32[2,64]{1,0:T(2,128)} %bitcast.3, bf16[64,128,1024]{2,1,0:T(8,128)(2,1)} %integrals.1, bf16[64,128,128]{2,1,0:T(8,128)(2,1)} %metric.1, bf16[96,1024]{1,0:T(8,128)(2,1)} %density.1), custom_call_target="tpu_custom_call" | custom-call | tf_op jit(solution)/shard_map/exchange/pallas_call | solution.py:303
  56.6 1.8 %copy.7 = f32[96,1024]{1,0:T(8,128)} copy(f32[96,1024]{1,0:T(8,128)} %exchange.1) | data formatting | bytes 786432

commit v3 on v2

--- a/solution.py
+++ b/solution.py
@@ -115,9 +115,9 @@
 
 def exchange_kernel(
     owners, atoms, integrals, metric, density, total,
-    owner_ref, atom_ref, tables, scalars, req, dens, outgoing, landed, outbox, returned, rows32, chosen,
+    owner_ref, atom_ref, tables, scalars, req, dens, outgoing, landed, outbox, returned, rows32, chosen, summed,
     q_buf, m_buf, z_ref, fw, qw, x_even, r_even, x_odd, r_odd, e1_even, e2_even, e1_odd, e2_odd, terms,
-    sems, index_sems, q_sems, m_sems,
+    sems, out_sems, index_sems, q_sems, m_sems,
 ):
     me = my_index()
 
@@ -195,17 +195,16 @@
     onehots = [jnp.where(local_atom == atom, 1.0, 0.0) for atom in (first, last)]
     for c in range(2):
         picks = onehots[c][:, :ATOMS].astype(BF16)
+        picked = jnp.dot(picks, dens[...], preferred_element_type=F32)
         for part in range(8):
-            rows32[pl.ds(8 * c + part, DEVS, stride=BOX), :] = jnp.dot(
-                picks, dens[:, part * 128 : (part + 1) * 128], preferred_element_type=F32
-            )
+            rows32[pl.ds(8 * c + part, DEVS, stride=BOX), :] = picked[:, part * 128 : (part + 1) * 128]
 
     def answer(t):
         outgoing[t] = rows32[pl.ds(pl.multiple_of(t * BOX, 8), 16), :].astype(BF16)
 
     start_swap(me, outgoing, landed, sems.at[2], sems.at[3], answer)
     for c in range(2):
-        chosen[c] = onehots[c].T.astype(BF16)
+        chosen[:, c * DEVS : (c + 1) * DEVS] = onehots[c].T.astype(BF16)
     table_copy.wait()
     lax.fori_loop(EARLY, GROUPS, fit, 0)
     wait_received(landed, sems.at[3])
@@ -270,7 +269,8 @@
         apply(g + 2, e1_even, e2_even, x_even, r_even)
         return carry
 
-    lax.fori_loop(0, GROUPS // 2 - 1, two_groups, 0)
+    lax.fori_loop(0, GROUPS // 2 - 2, two_groups, 0, unroll=2)
+    two_groups(GROUPS // 2 - 2, 0)
     expand(GROUPS - 1, e1_odd, e2_odd)
     contract(GROUPS - 2, x_even, r_even)
     apply(GROUPS - 1, e1_odd, e2_odd, x_odd, r_odd)
@@ -281,22 +281,27 @@
 
     start_swap(me, outbox, returned, sems.at[6], sems.at[7], box)
     wait_received(returned, sems.at[7])
+
+    def out_copy(part):
+        columns = pl.ds(part * 128, 128)
+        return pltpu.make_async_copy(summed.at[:, columns], total.at[:, columns], out_sems.at[part])
+
     for t in range(DEVS):
         rows32[t * BOX : t * BOX + 16, :] = returned[t].astype(F32)
     for part in range(8):
-        acc = None
-        for c in range(2):
-            tile = rows32[pl.ds(8 * c + part, DEVS, stride=BOX), :].astype(BF16)
-            term = jnp.dot(chosen[c, :ATOMS, :], tile, preferred_element_type=F32)
-            acc = term if acc is None else acc + term
-        total[:, part * 128 : (part + 1) * 128] = acc
+        tiles = [rows32[pl.ds(8 * c + part, DEVS, stride=BOX), :].astype(BF16) for c in range(2)]
+        summed[:, part * 128 : (part + 1) * 128] = jnp.dot(
+            chosen[:ATOMS, :], jnp.concatenate(tiles, axis=0), preferred_element_type=F32
+        )
+        out_copy(part).start()
+    for part in range(8):
+        out_copy(part).wait()
     wait_sent(req, sems.at[1])
     wait_sent(outgoing, sems.at[2])
     wait_sent(outbox, sems.at[6])
 
 
 def local(pair_owner, pair_atom, integrals, metric_inverse, density):
-    vmem = pl.BlockSpec(memory_space=pltpu.VMEM)
     hbm = pl.BlockSpec(memory_space=pltpu.HBM)
     boxes = pltpu.VMEM((DEVS, 16, 128), BF16)
     wide = (GROUP * NB, NB * NFIT)
@@ -304,7 +309,7 @@
         exchange_kernel,
         out_shape=jax.ShapeDtypeStruct((ATOMS, NB * NB), F32),
         in_specs=[hbm] * 5,
-        out_specs=vmem,
+        out_specs=hbm,
         scratch_shapes=[
             pltpu.VMEM((2, PAIRS), jnp.int32),
             pltpu.VMEM((2, PAIRS), jnp.int32),
@@ -314,7 +319,8 @@
             pltpu.VMEM((ATOMS, NB * NB), BF16),
             boxes, boxes, boxes, boxes,
             pltpu.VMEM((DEVS * BOX, 128), F32),
-            pltpu.VMEM((2, 128, DEVS), BF16),
+            pltpu.VMEM((128, 2 * DEVS), BF16),
+            pltpu.VMEM((ATOMS, NB * NB), F32),
             pltpu.VMEM((BUFFERS, GROUP, NFIT, NB * NB), BF16),
             pltpu.VMEM((BUFFERS, GROUP, NFIT, NFIT), BF16),
             pltpu.VMEM((GROUP, NB * PITCH, 128), F32),
@@ -323,6 +329,7 @@
             *[pltpu.VMEM(wide, BF16)] * 4,
             *[pltpu.VMEM((GROUP, NB, 256), F32)] * 4,
             pltpu.VMEM((2 * PAIRS + 1, 8, 128), F32),
+            pltpu.SemaphoreType.DMA((8,)),
             pltpu.SemaphoreType.DMA((8,)),
             pltpu.SemaphoreType.DMA((2,)),
             pltpu.SemaphoreType.DMA((BUFFERS,)),

time: 58.5 us -> 57.9 us (0.990)
  Pallas kernels: 56.6 us -> 56 us
    pallas_call x1, Pallas kernels: 56.6 us -> 56 us  [local(): pl.pallas_call(exchange_kernel, out_shape=jax.ShapeDtypeStruct((ATOMS, NB...]
where the time goes in v3:
time: 57.9 us; the launch traced here: 57.8 us
  Pallas kernels  56 us (97%)
  local copies, waits for them, and re-layouts  1.77 us (3%)
    pallas_call x1, Pallas kernels, local(): pl.pallas_call(exchange_kernel, out_shape=jax.ShapeDtypeStruct((ATOMS, NB...  56 us
    unnamed x1, local copies, waits for them, and re-layouts  1.77 us

profile of v3, /device:TPU:1, one launch (start us, length us, event | category | flops | bytes accessed | tf_op | source)
XLA Modules:
  0.0 57.8 jit_solution(14183860133841954738)
XLA Ops:
  0.0 56.0 %exchange.1 = f32[96,1024]{1,0:T(8,128)} custom-call(s32[2,64]{1,0:T(2,128)} %bitcast.2, s32[2,64]{1,0:T(2,128)} %bitcast.3, bf16[64,128,1024]{2,1,0:T(8,128)(2,1)} %integrals.1, bf16[64,128,128]{2,1,0:T(8,128)(2,1)} %metric.1, bf16[96,1024]{1,0:T(8,128)(2,1)} %density.1), custom_call_target="tpu_custom_call" | custom-call | tf_op jit(solution)/shard_map/exchange/pallas_call | solution.py:308
  56.0 1.8 %copy.7 = f32[96,1024]{1,0:T(8,128)} copy(f32[96,1024]{1,0:T(8,128)} %exchange.1) | data formatting | bytes 786432
